TPU v7x, 256 devices: a whole 4x4x8 slice. The times are simulated.
256 devices in a mesh: tier: 16 (over z, core), serve: 4 (over y), head: 4 (over x).
Axes of the slice: x: 4, y: 4, z: 8, core: 2. Of those that a mesh axis runs over, the one named last changes fastest.
Arguments:
- passage_ids: int32 [16, 16], replicated, may hold values from 0 to 63, as said below
- location: int32 [64], replicated, may hold values from 0 to 63, as said below
- passage_len: int32 [64], replicated, may hold values from 128 to 256, as said below
- hit: int32 [64], P('tier'), may hold values from 0 to 1, as said below
- sel_index: int32 [16, 16, 64], P('tier'), may hold values from 0 to 255, as said below
- sel_hidden: bfloat16 [16, 1024, 8192], P('tier', None, ('serve', 'head')), may hold values from -6 to 40
- miss_hidden: bfloat16 [16, 256, 8192], P('tier', None, 'serve'), may hold values from -6 to 6
- w_qkv: bfloat16 [8192, 5120], P('serve', 'head'), may hold values from -1 to 1
- cache: bfloat16 [64, 2, 256, 512], P('tier', None, None, 'head'), may hold values from -6 to 11
Outputs:
- attended: bfloat16 [16, 16, 64, 4096], P('tier', 'serve', None, 'head')
Inputs may be any that keep to these rules, and one draw needn't show every extreme that they name: `passage_ids`: within a request all ids differ; at most 2 of a request's passages are stored at one owner (location // 4), and in every request exactly 2 of them are at some owner. `location`: a permutation of the storage positions. `passage_len`: some passage has all 256 tokens live. `hit`: each owner's 4 storage positions hold exactly 1 zeros. `sel_index`: strictly increasing along the last dimension, each below the passage's live length.
All inputs are finite; a program needn't handle non-finite values.
Results may differ from a plain program's by a relative error of at most 0.018.
Values may be sent and summed in bfloat16 or wider, within the bound.
A program may use at most 128 MiB of HBM per device.

v0:
```python
import math

import jax
import jax.numpy as jnp
from jax import lax
from jax.sharding import PartitionSpec as P

HD = 128
G = 8
PLEN = 256
SEL = 64
NPAS = 16


def rope_parts(positions):
    half_index = jnp.arange(HD // 2, dtype=jnp.float32)
    inverse = jnp.exp(half_index * (-2.0 * math.log(500000.0) / HD))
    angle_table = positions.astype(jnp.float32)[..., None] * inverse
    return (jnp.cos(angle_table), jnp.sin(angle_table))


def rotate(values, cosine, sine_part):
    front_half = values[..., : HD // 2]
    back_half = values[..., HD // 2 :]
    return jnp.concatenate(
        [front_half * cosine - back_half * sine_part, back_half * cosine + front_half * sine_part],
        axis=-1,
    )


def finish_kv(summed, positions, kv_count):
    rows_count = summed.shape[0]
    span_rows = summed.shape[1]
    row_width = kv_count * HD
    key_part = summed[..., :row_width].reshape(rows_count, span_rows, kv_count, HD)
    cosine, sine_part = rope_parts(positions)
    rotated = rotate(key_part, cosine[None, :, None, :], sine_part[None, :, None, :])
    rotated = rotated.reshape(rows_count, span_rows, row_width).astype(jnp.bfloat16)
    value_part = summed[..., row_width:].astype(jnp.bfloat16)
    return jnp.stack([rotated, value_part], axis=1)


def local(
    passage_ids, location, passage_len, hit, sel_index, sel_hidden, miss_hidden, w_qkv, cache
):
    servers = lax.axis_size("serve")
    me_tier = lax.axis_index("tier")
    me_serve = lax.axis_index("serve")
    row_width = cache.shape[3]
    kv_dev = row_width // HD
    miss_count = miss_hidden.shape[0]
    local_d = w_qkv.shape[0]
    weights = w_qkv.reshape(local_d, kv_dev, G + 2, HD)
    kv_weight = jnp.transpose(weights[:, :, G:, :], (0, 2, 1, 3)).reshape(local_d, 2 * row_width)
    partial_kv = jnp.dot(
        miss_hidden.reshape(-1, local_d), kv_weight, preferred_element_type=jnp.float32
    )
    partial_kv = partial_kv.reshape(miss_count, PLEN, 2 * row_width)
    summed = lax.psum(partial_kv.astype(jnp.bfloat16), "serve").astype(jnp.float32)
    encoded = finish_kv(summed, jnp.arange(PLEN, dtype=jnp.int32), kv_dev)
    missing = jnp.argsort(hit, stable=True)[:miss_count]
    kv_store = cache.at[missing].set(encoded)
    request_ids = passage_ids[me_tier]
    stored_all = location[passage_ids]
    wanted = stored_all[me_tier]
    empty_blocks = jnp.zeros((NPAS, 2, PLEN, row_width), jnp.bfloat16)
    shard_rows = lax.all_gather(kv_store, "tier", axis=0, tiled=True)
    shard_len = shard_rows.shape[0]
    inside = (wanted >= 0) & (wanted < shard_len)
    picked = jnp.take(shard_rows, jnp.clip(wanted, 0, shard_len - 1), axis=0)
    blocks = jnp.where(inside[:, None, None, None], picked, empty_blocks)
    hidden_rows = lax.all_gather(sel_hidden[0], "head", axis=1, tiled=True)
    rows_dev = NPAS * SEL // servers
    mine_rows = lax.psum_scatter(
        jnp.dot(hidden_rows, w_qkv, preferred_element_type=jnp.float32),
        "serve",
        scatter_dimension=0,
        tiled=True,
    ).astype(jnp.bfloat16)
    mine_rows = mine_rows.reshape(rows_dev, kv_dev, G + 2, HD)
    lengths = passage_len[request_ids]
    offsets = jnp.cumsum(lengths) - lengths
    chosen = sel_index[0]
    positions = offsets[:, None] + chosen
    per_dev = NPAS // servers
    my_pos = lax.dynamic_slice_in_dim(positions, me_serve * per_dev, per_dev, 0).reshape(-1)
    cosine, sine_part = rope_parts(my_pos)
    queries = rotate(
        mine_rows[:, :, :G].astype(jnp.float32),
        cosine[:, None, None, :],
        sine_part[:, None, None, :],
    ).astype(jnp.bfloat16)
    fresh_keys = rotate(
        mine_rows[:, :, G].astype(jnp.float32), cosine[:, None, :], sine_part[:, None, :]
    ).astype(jnp.bfloat16)
    fresh_vals = mine_rows[:, :, G + 1]
    fresh_pair = jnp.stack(
        [fresh_keys.reshape(rows_dev, row_width), fresh_vals.reshape(rows_dev, row_width)]
    )
    fresh_all = lax.all_gather(fresh_pair, "serve", axis=1, tiled=True)
    cached_keys = blocks[:, 0].astype(jnp.float32).reshape(NPAS, PLEN, kv_dev, HD)
    shift_cos, shift_sin = rope_parts(offsets)
    moved_keys = rotate(cached_keys, shift_cos[:, None, None, :], shift_sin[:, None, None, :])
    moved_keys = moved_keys.astype(jnp.bfloat16).reshape(NPAS, PLEN, row_width)
    passage_index = jnp.arange(NPAS, dtype=jnp.int32)[:, None]
    key_table = moved_keys.at[passage_index, chosen].set(fresh_all[0].reshape(NPAS, SEL, row_width))
    value_table = (
        blocks[:, 1].at[passage_index, chosen].set(fresh_all[1].reshape(NPAS, SEL, row_width))
    )
    key_rows = key_table.reshape(NPAS * PLEN, kv_dev, HD)
    value_rows = value_table.reshape(NPAS * PLEN, kv_dev, HD)
    key_passage = jnp.arange(NPAS * PLEN, dtype=jnp.int32) // PLEN
    key_slot = jnp.arange(NPAS * PLEN, dtype=jnp.int32) % PLEN
    query_passage = me_serve * per_dev + jnp.arange(rows_dev, dtype=jnp.int32) // SEL
    query_slot = lax.dynamic_slice_in_dim(chosen, me_serve * per_dev, per_dev, 0).reshape(-1)
    live = key_slot < lengths[key_passage]
    before = key_passage[None, :] < query_passage[:, None]
    same_part = (key_passage[None, :] == query_passage[:, None]) & (
        key_slot[None, :] <= query_slot[:, None]
    )
    allowed = live[None, :] & (before | same_part)
    scale = 1.0 / math.sqrt(HD)
    head_block = max(1, min(G, 512 // rows_dev))
    while G % head_block:
        head_block -= 1
    block_count = G // head_block
    query_blocks = jnp.moveaxis(
        queries.reshape(rows_dev, kv_dev, block_count, head_block, HD), 2, 0
    )

    def attend(query_part):
        scores = (
            jnp.einsum("qhgd,khd->hgqk", query_part, key_rows, preferred_element_type=jnp.float32)
            * scale
        )
        scores = jnp.where(allowed[None, None], scores, -jnp.inf)
        row_top = jnp.max(scores, axis=-1, keepdims=True)
        expo_terms = jnp.exp(scores - row_top)
        probs = (expo_terms / jnp.sum(expo_terms, axis=-1, keepdims=True)).astype(jnp.bfloat16)
        mixed = jnp.einsum("hgqk,khd->qhgd", probs, value_rows, preferred_element_type=jnp.float32)
        return mixed.astype(jnp.bfloat16)

    attended = lax.map(attend, query_blocks)
    attended = jnp.moveaxis(attended, 0, 2).reshape(per_dev, SEL, kv_dev * G * HD)
    return attended[None]


def solution(mesh):
    in_specs = (
        P(),
        P(),
        P(),
        P("tier"),
        P("tier", None, None),
        P("tier", None, ("serve", "head")),
        P("tier", None, "serve"),
        P("serve", "head"),
        P("tier", None, None, "head"),
    )
    out_specs = P("tier", "serve", None, "head")
    return jax.shard_map(local, mesh=mesh, in_specs=in_specs, out_specs=out_specs, check_vma=False)
```

profile of v0, /device:TPU:24, one launch (start us, length us, event | category | flops | bytes accessed | tf_op | source)
XLA Modules:
  0.0 224.9 jit_solution(1049261223859262809)
XLA Ops:
  7.4 1.1 copy.64
  8.5 7.9 %copy.42 = bf16[2048,1280]{0,1:T(8,128)(2,1)} copy(bf16[2048,1280]{1,0:T(8,128)(2,1)} %param.20) | data formatting | bytes 10485760 | tf_op args[7]
  16.4 1.3 slice.128
  17.8 1.1 fusion.21
  21.4 45.5 %all-reduce.2.cloned.1.call-done = bf16[1,256,256]{1,2,0:T(8,128)(2,1)} async-done(((bf16[1,256,256]{1,2,0:T(8,128)(2,1)}), bf16[1,256,256]{1,2,0:T(8,128)(2,1)}) %all-reduce.2.cloned.1.call-update) | async-done | bytes 131088 | tf_op jit(solution)/shard_map/psum | solution.py:59
  66.9 0.9 fusion.43
  69.9 4.8 %all-gather.6.cloned.1.call-done = bf16[1,1024,2048]{2,1,0:T(8,128)(2,1)} async-done(((bf16[1,1024,512]{2,1,0:T(8,128)(2,1)}), bf16[1,1024,2048]{2,1,0:T(8,128)(2,1)}) %all-gather.6.cloned.1.call-update) | async-done | bytes 4194320 | tf_op jit(solution)/shard_map/all_gather | solution.py:72
  74.7 10.5 %fusion.19 = f32[1024,1280]{1,0:T(8,128)} fusion(bf16[2048,1280]{1,0:T(8,128)(2,1)} %param.20, bf16[1,1024,2048]{2,1,0:T(8,128)(2,1)} %all-gather.6.cloned.1.call-done), kind=kOutput, calls=%fused_computation.21 | convolution fusion | flops 5368709120 | bytes 14680064 | tf_op jit(solution)/shard_map/dot_general | solution.py:75
  87.2 1.9 gather_fusion.1
  90.9 4.3 %compare_select_fusion.1 = s32[4096,1]{0,1:T(1,128)S(1)} fusion(s32[]{:T(128)} %bitcast.47, s32[]{:T(128)} %bitcast.48, s32[]{:T(128)} %bitcast.49, s32[]{:T(128)} %bitcast.50, s32[]{:T(128)} %bitcast.51, s32[]{:T(128)} %bitcast.53, s32[]{:T(128)} %bitcast.52), kind=kLoop, calls=%fused_computation.81 | loop fusion | flops 94208 | bytes 16412 | tf_op jit(solution)/shard_map/gather | solution.py:116
  95.3 5.8 %select_compare_fusion = pred[4096]{0:T(1024)(128)(4,1)S(1)} fusion(pred[4096]{0:T(1024)(128)(4,1)S(1)} %compare_reduce_fusion, pred[4096]{0:T(1024)(128)(4,1)S(1)} %compare_reduce_fusion.1, pred[4096]{0:T(1024)(128)(4,1)S(1)} %compare_reduce_fusion.2, pred[4096]{0:T(1024)(128)(4,1)S(1)} %compare_reduce_fusion.3, ...), kind=kLoop, calls=%fused_computation.101 | loop fusion | flops 65536 | bytes 57380 | tf_op jit(solution)/shard_map/lt | solution.py:116
  101.1 0.9 multiply_cosine_fusion.2
  102.0 30.8 %all-gather.4.cloned.1.call-done = bf16[64,2,256,128]{3,2,1,0:T(8,128)(2,1)} async-done(((bf16[4,2,256,128]{3,2,1,0:T(8,128)(2,1)}), bf16[64,2,256,128]{3,2,1,0:T(8,128)(2,1)}) %all-gather.4.cloned.1.call-update) | async-done | bytes 8388624 | tf_op jit(solution)/shard_map/all_gather | solution.py:67
  132.8 4.4 %gather_fusion.2 = bf16[16,2,256,128]{3,2,1,0:T(8,128)(2,1)S(1)} fusion(bf16[64,2,256,128]{3,2,1,0:T(8,128)(2,1)} %all-gather.4.cloned.1.call-done, s32[1024]{0:T(1024)S(1)} %pad_clamp_fusion), kind=kCustom, calls=%fused_computation.2 | custom fusion | bytes 4194368 | tf_op jit(solution)/shard_map/jit(_take)/gather | solution.py:70
  137.8 0.9 fusion.22
  139.3 2.5 %reduce-scatter.2.cloned.1.call-done = f32[256,1280]{1,0:T(8,128)} async-done(((f32[1024,1280]{1,0:T(8,128)}), f32[256,1280]{1,0:T(8,128)}) %reduce-scatter.2.cloned.1.call-update) | async-done | bytes 1310736 | tf_op jit(solution)/shard_map/reduce_scatter | solution.py:74
  141.8 2.2 convert_element_type.123
  144.0 2.2 copy.38
  146.2 0.9 fusion.42
  147.1 2.1 slice_convert_fusion
  149.5 12.8 %all_gather.11 = bf16[2,1024,128]{1,2,0:T(8,128)(2,1)S(1)} all-gather(bf16[2,256,128]{1,2,0:T(8,128)(2,1)S(1)} %pad_maximum_fusion.1), channel_id=1, replica_groups=mesh['tier'=16,'serve'=4,'head'=4] {'serve'}, dimensions={1}, use_global_device_ids=true | all-gather | bytes 655360 | tf_op jit(solution)/shard_map/all_gather | solution.py:100
  163.1 0.8 copy.47
  163.9 1.1 copy.46
  165.0 2.2 subtract_convert_fusion.1
  167.2 2.0 copy.40
  169.2 2.0 copy.41
  171.1 4.1 %scatter_fusion.1 = bf16[4096,128]{1,0:T(8,128)(2,1)S(1)} fusion(bf16[4096,128]{1,0:T(8,128)(2,1)S(1)} %bitcast.146, s32[1024]{0:T(1024)S(1)} %reshape.804, bf16[1024,128]{1,0:T(8,128)(2,1)} %copy.47), kind=kCustom, calls=%fused_computation.4 | custom fusion | bytes 790528
  175.3 3.9 %scatter_fusion = bf16[4096,128]{1,0:T(8,128)(2,1)S(1)} fusion(bf16[4096,128]{1,0:T(8,128)(2,1)S(1)} %bitcast.148, s32[1024]{0:T(1024)S(1)} %reshape.804, bf16[1024,128]{1,0:T(8,128)(2,1)S(1)} %copy.46), kind=kCustom, calls=%fused_computation.3 | custom fusion | bytes 790528
  179.2 2.3 %maximum_bitcast_fusion = bf16[4,256,1,2,128]{4,1,3,2,0:T(8,128)(2,1)} fusion(bf16[256,1,4,2,64]{4,0,3,1,2:T(8,128)(2,1)} %copy.41, bf16[256,1,4,2,64]{4,0,3,1,2:T(8,128)(2,1)} %copy.40), kind=kLoop, calls=%fused_computation.35 | loop fusion | flops 1048576 | bytes 1048576 | tf_op jit(solution)/shard_map/transpose | solution.py:127
  181.5 33.2 %while.12 = (s32[]{:T(128)}, bf16[4,256,1,2,128]{4,1,3,2,0:T(8,128)(2,1)}, bf16[4,256,1,2,128]{4,1,3,2,0:T(8,128)(2,1)}, bf16[4096,1,128]{2,0,1:T(8,128)(2,1)S(1...) while((s32[]{:T(128)}, ...), condition=%wide.region_10.11_spmd.clone, body=%wide.region_7.10_spmd.clone.sunk | while | flops 1096875008 | bytes 29672556 | solution.py:143
  181.5 1.6 or_and_fusion.2
  183.1 2.7 %fusion.69 = (f32[2,256]{1,0:T(2,128)S(1)}, f32[1,2,256,4096]{3,2,1,0:T(8,128)S(1)}) fusion(bf16[4096,1,128]{2,0,1:T(8,128)(2,1)S(1)} %get-tuple-element.231, bf16[4,256,1,2,128]{4,1,3,2,0:T(8,128)(2,1)} %get-tuple-element.230, s32[]{:T(128)} %get-tuple-element.217, pred[256,4096]{1,0:T(8,128)(4,1)S(1)} %or_and_fusion.2), kind=kOutput, calls=%fused_computation.139.clone.1 | convolution fusion | flops 543161856 | bytes 10619392 | tf_op jit(solution)/shard_map/while/body/eval_jaxpr/qhgd,khd->hgqk/dot_general | solution.py:133
  185.8 1.3 fusion.70
  187.1 2.7 %fusion.71 = bf16[4,256,1,2,128]{4,1,3,2,0:T(8,128)(2,1)} fusion(bf16[4,256,1,2,128]{4,1,3,2,0:T(8,128)(2,1)} %get-tuple-element.218, s32[]{:T(128)} %get-tuple-element.217, f32[2,256]{1,0:T(2,128)S(1)} %fusion.70, f32[1,2,256,4096]{3,2,1,0:T(8,128)S(1)} %get-tuple-element.204, f32[2,256]{1,0:T(2,128)S(1)} %get-tuple-element.205, ...), kind=kOutput, calls=%fused_computation.15.clone.1 | convolution fusion | flops 543227904 | bytes 9572864 | tf_op jit(solution)/shard_map/while/body/eval_jaxpr/hgqk,khd->qhgd/dot_general | solution.py:140
  189.8 1.6 or_and_fusion.2
  191.4 2.7 %fusion.69 = (f32[2,256]{1,0:T(2,128)S(1)}, f32[1,2,256,4096]{3,2,1,0:T(8,128)S(1)}) fusion(bf16[4096,1,128]{2,0,1:T(8,128)(2,1)S(1)} %get-tuple-element.231, bf16[4,256,1,2,128]{4,1,3,2,0:T(8,128)(2,1)} %get-tuple-element.230, s32[]{:T(128)} %get-tuple-element.217, pred[256,4096]{1,0:T(8,128)(4,1)S(1)} %or_and_fusion.2), kind=kOutput, calls=%fused_computation.139.clone.1 | convolution fusion | flops 543161856 | bytes 10619392 | tf_op jit(solution)/shard_map/while/body/eval_jaxpr/qhgd,khd->hgqk/dot_general | solution.py:133
  194.1 1.3 fusion.70
  195.4 2.7 %fusion.71 = bf16[4,256,1,2,128]{4,1,3,2,0:T(8,128)(2,1)} fusion(bf16[4,256,1,2,128]{4,1,3,2,0:T(8,128)(2,1)} %get-tuple-element.218, s32[]{:T(128)} %get-tuple-element.217, f32[2,256]{1,0:T(2,128)S(1)} %fusion.70, f32[1,2,256,4096]{3,2,1,0:T(8,128)S(1)} %get-tuple-element.204, f32[2,256]{1,0:T(2,128)S(1)} %get-tuple-element.205, ...), kind=kOutput, calls=%fused_computation.15.clone.1 | convolution fusion | flops 543227904 | bytes 9572864 | tf_op jit(solution)/shard_map/while/body/eval_jaxpr/hgqk,khd->qhgd/dot_general | solution.py:140
  198.1 1.6 or_and_fusion.2
  199.7 2.7 %fusion.69 = (f32[2,256]{1,0:T(2,128)S(1)}, f32[1,2,256,4096]{3,2,1,0:T(8,128)S(1)}) fusion(bf16[4096,1,128]{2,0,1:T(8,128)(2,1)S(1)} %get-tuple-element.231, bf16[4,256,1,2,128]{4,1,3,2,0:T(8,128)(2,1)} %get-tuple-element.230, s32[]{:T(128)} %get-tuple-element.217, pred[256,4096]{1,0:T(8,128)(4,1)S(1)} %or_and_fusion.2), kind=kOutput, calls=%fused_computation.139.clone.1 | convolution fusion | flops 543161856 | bytes 10619392 | tf_op jit(solution)/shard_map/while/body/eval_jaxpr/qhgd,khd->hgqk/dot_general | solution.py:133
  202.4 1.3 fusion.70
  203.7 2.7 %fusion.71 = bf16[4,256,1,2,128]{4,1,3,2,0:T(8,128)(2,1)} fusion(bf16[4,256,1,2,128]{4,1,3,2,0:T(8,128)(2,1)} %get-tuple-element.218, s32[]{:T(128)} %get-tuple-element.217, f32[2,256]{1,0:T(2,128)S(1)} %fusion.70, f32[1,2,256,4096]{3,2,1,0:T(8,128)S(1)} %get-tuple-element.204, f32[2,256]{1,0:T(2,128)S(1)} %get-tuple-element.205, ...), kind=kOutput, calls=%fused_computation.15.clone.1 | convolution fusion | flops 543227904 | bytes 9572864 | tf_op jit(solution)/shard_map/while/body/eval_jaxpr/hgqk,khd->qhgd/dot_general | solution.py:140
  206.4 1.6 or_and_fusion.2
  208.0 2.7 %fusion.69 = (f32[2,256]{1,0:T(2,128)S(1)}, f32[1,2,256,4096]{3,2,1,0:T(8,128)S(1)}) fusion(bf16[4096,1,128]{2,0,1:T(8,128)(2,1)S(1)} %get-tuple-element.231, bf16[4,256,1,2,128]{4,1,3,2,0:T(8,128)(2,1)} %get-tuple-element.230, s32[]{:T(128)} %get-tuple-element.217, pred[256,4096]{1,0:T(8,128)(4,1)S(1)} %or_and_fusion.2), kind=kOutput, calls=%fused_computation.139.clone.1 | convolution fusion | flops 543161856 | bytes 10619392 | tf_op jit(solution)/shard_map/while/body/eval_jaxpr/qhgd,khd->hgqk/dot_general | solution.py:133
  210.7 1.3 fusion.70
  212.0 2.7 %fusion.71 = bf16[4,256,1,2,128]{4,1,3,2,0:T(8,128)(2,1)} fusion(bf16[4,256,1,2,128]{4,1,3,2,0:T(8,128)(2,1)} %get-tuple-element.218, s32[]{:T(128)} %get-tuple-element.217, f32[2,256]{1,0:T(2,128)S(1)} %fusion.70, f32[1,2,256,4096]{3,2,1,0:T(8,128)S(1)} %get-tuple-element.204, f32[2,256]{1,0:T(2,128)S(1)} %get-tuple-element.205, ...), kind=kOutput, calls=%fused_computation.15.clone.1 | convolution fusion | flops 543227904 | bytes 9572864 | tf_op jit(solution)/shard_map/while/body/eval_jaxpr/hgqk,khd->qhgd/dot_general | solution.py:140
  214.7 1.6 copy.48
  216.3 1.2 broadcast_in_dim_reshape.4
  (86 shorter events, 10.3 us)
Async XLA Ops:
  7.4 10.4 %copy-start = (bf16[1,256,2048]{2,1,0:T(8,128)(2,1)S(1)}, bf16[1,256,2048]{2,1,0:T(8,128)(2,1)}, u32[]{:S(2)}) copy-start(bf16[1,256,2048]{2,1,0:T(8,128)(2,1)} %param.19) | copy-start | bytes 3145732
  7.4 59.5 %all-reduce.2.cloned.1.call-start = ((), (), s32[]{:S(2)}) async-start(), calls=%async_computation.2 | async-start | bytes 262144 | tf_op jit(solution)/shard_map/psum | solution.py:59
  16.4 3.1 %copy-start.9 = (s32[4]{0:T(128)S(1)}, s32[4]{0:T(128)}, u32[]{:S(2)}) copy-start(s32[4]{0:T(128)} %param.16) | copy-start | bytes 52
  16.4 4.2 %copy-start.8 = (s32[4]{0:T(128)S(1)}, s32[4]{0:T(128)}, u32[]{:S(2)}) copy-start(s32[4]{0:T(128)} %constant.130.clone.1) | copy-start | bytes 52
  18.9 55.8 %all-gather.6.cloned.1.call-start = ((), (), s32[]{:S(2)}) async-start(), calls=%async_computation.4 | async-start | bytes 5242880 | tf_op jit(solution)/shard_map/all_gather | solution.py:72
  19.5 113.3 %all-gather.4.cloned.1.call-start = ((), (), s32[]{:S(2)}) async-start(), calls=%async_computation.3 | async-start | bytes 8912896 | tf_op jit(solution)/shard_map/all_gather | solution.py:67
  69.0 0.8 copy-start.3
  69.8 71.9 %reduce-scatter.2.cloned.1.call-start = ((), (), s32[]{:S(2)}) async-start(), calls=%async_computation.1 | async-start | bytes 6553600 | tf_op jit(solution)/shard_map/reduce_scatter | solution.py:74
  85.2 0.7 copy-start.5
  85.2 0.7 copy-start.2
  85.2 1.7 copy-start.4
  85.2 2.0 copy-start.1
  87.1 2.0 copy-start.7
  87.1 2.1 copy-start.6
Sparse Core Ops, SparseCore 0:
  19.0 47.8 all-reduce.1
  85.3 56.4 reduce-scatter.1
Sparse Core Ops, SparseCore 1:
  21.3 53.3 all-gather.5
  76.5 56.2 all-gather.3
where the time goes:
time: 229 us; the launch traced here: 225 us
  waiting for transfers between devices  84.2 us (37%)
  local copies, waits for them, and re-layouts  40 us (17%)
  other arithmetic  39.1 us (17%)
  matrix products  33.4 us (15%)
  between operations  15.3 us (7%)
  blocking collectives  12.8 us (6%)
    psum x1, waiting for transfers between devices, local(): lax.psum(partial_kv.astype(jnp.bfloat16), 'serve').astype(jnp.float32)  45.5 us
    all_gather x1, waiting for transfers between devices, local(): shard_rows = lax.all_gather(kv_store, 'tier', axis=0, tiled=True)  30.8 us
    unnamed x26, local copies, waits for them, and re-layouts  18.8 us
    all_gather x1, blocking collectives, local(): fresh_all = lax.all_gather(fresh_pair, 'serve', axis=1, tiled=True)  12.8 us
    dot_general x4, matrix products, attend(): jnp.einsum('hgqk,khd->qhgd', probs, value_rows, preferred_element_type=jn...  10.9 us
    dot_general x4, matrix products, attend(): jnp.einsum('qhgd,khd->hgqk', query_part, key_rows, preferred_element_type...  10.9 us
    dot_general x1, matrix products, local(): jnp.dot(hidden_rows, w_qkv, preferred_element_type=jnp.float32)  10.5 us
    and x4, other arithmetic, local(): allowed = live[None, :] & (before | same_part)  6.35 us
  transfers between devices with their start and end apart: 4, of which 4 were waited for; matrix products, arithmetic and copies ran while one was open for 16% of the time, Pallas kernels for 0%

commit v1 on v0

v1 whole, which is shorter than its diff:
```python
import functools
import math

import jax
import jax.numpy as jnp
from jax import lax
from jax.experimental import pallas as pl
from jax.experimental.pallas import tpu as pltpu
from jax.sharding import PartitionSpec as P

HD = 128
G = 8
PLEN = 256
SEL = 64
NPAS = 16
POWN = 4
NT = 16
NS = 4
ROWS = NPAS * SEL
COLS = (G + 2) * HD
CH = 4
CR = ROWS // CH
FEAT = 512
BF = jnp.bfloat16
F32 = jnp.float32
MESH = pl.DeviceIdType.MESH
LN_BASE = math.log(500000.0)
EXP_SCALE = math.log2(math.e) / math.sqrt(HD)


def remote(src, dst, ssem, rsem, target):
    return pltpu.make_async_remote_copy(
        src_ref=src, dst_ref=dst, send_sem=ssem, recv_sem=rsem, device_id=target, device_id_type=MESH
    )


def rope_rows(angle):
    lane = lax.broadcasted_iota(jnp.int32, angle.shape, 1)
    sine = jnp.sin(angle)
    return jnp.cos(angle), jnp.where(lane < HD // 2, -sine, sine)


def inv_freq(shape):
    lane = lax.broadcasted_iota(jnp.int32, shape, 1)
    half = jnp.where(lane < HD // 2, lane, lane - HD // 2).astype(F32)
    return jnp.exp(half * (-2.0 * LN_BASE / HD))


def rotate(x, c, s):
    return x * c + pltpu.roll(x, HD // 2, 1) * s


def kernel(
    pid_ref, loc_ref, len_ref, hit_ref, sel_ref, hid_ref, miss_ref, w_ref, cache_ref, out_ref,
    wv, mv, xb, zb, eb, er, pb, rb, fb, qb, ktab, vtab, ob, offs, oc, osn, rc, rsn, acc_s, m_s, l_s,
    lsem, xs, xr, es, ers, zs, zr, ss, sr, ps, pr, fs, fr, os_, or_,
):
    t = lax.axis_index("tier")
    s = lax.axis_index("serve")
    h = lax.axis_index("head")
    sib = {"tier": t + 1 - 2 * lax.rem(t, 2)}
    zright = {"tier": lax.rem(t + 2, NT)}
    zleft = {"tier": lax.rem(t + NT - 2, NT)}
    xright = {"head": lax.rem(h + 1, 4)}
    xleft = {"head": lax.rem(h + 3, 4)}

    def ydev(d):
        return {"serve": lax.rem(s + d, NS)}

    loads = [
        pltpu.make_async_copy(hid_ref, xb.at[0], lsem.at[0]),
        pltpu.make_async_copy(miss_ref, mv, lsem.at[1]),
        pltpu.make_async_copy(w_ref, wv, lsem.at[2]),
        pltpu.make_async_copy(cache_ref, zb.at[pl.ds(t * POWN, POWN)], lsem.at[3]),
    ]
    for cp in loads:
        cp.start()

    bar = pltpu.get_barrier_semaphore()
    partners = [xright, xleft, ydev(1), ydev(2), ydev(3), zright, zleft, sib]
    for dev in partners:
        pl.semaphore_signal(bar, inc=1, device_id=dev, device_id_type=MESH)
    pl.semaphore_wait(bar, len(partners))

    def x_own(c):
        rows = pl.ds(c * CR, CR)
        return (
            remote(xb.at[0, rows], xb.at[1, rows], xs.at[0, c], xr.at[0, c], xright),
            remote(xb.at[0, rows], xb.at[2, rows], xs.at[1, c], xr.at[1, c], xleft),
        )

    def x_fwd(c):
        a, b = pl.ds(c * CR, CR // 2), pl.ds(c * CR + CR // 2, CR // 2)
        return (
            remote(xb.at[1, a], xb.at[3, a], xs.at[2, c], xr.at[2, c], xright),
            remote(xb.at[2, b], xb.at[3, b], xs.at[3, c], xr.at[3, c], xleft),
        )

    loads[0].wait()
    for c in range(2):
        for cp in x_own(c):
            cp.start()

    total = jnp.int32(0)
    row_id = lax.broadcasted_iota(jnp.int32, (NPAS, HD), 0)
    off_rows = jnp.zeros((NPAS, HD), jnp.int32)
    for j in range(NPAS):
        offs[j] = total
        off_rows = jnp.where(row_id == j, total, off_rows)
        total = total + len_ref[pid_ref[t, j]]
    cosv, sinv = rope_rows(off_rows.astype(F32) * inv_freq((NPAS, HD)))
    oc[...] = cosv
    osn[...] = sinv

    loads[1].wait()
    loads[2].wait()
    eb[...] = jnp.dot(mv[...], wv[:, G * HD :], preferred_element_type=F32).astype(BF)
    enc = [remote(eb, er.at[d - 1], es.at[d - 1], ers.at[d - 1], ydev(d)) for d in (1, 2, 3)]
    for cp in enc:
        cp.start()

    eye = lax.broadcasted_iota(jnp.int32, (SEL, SEL), 0) == lax.broadcasted_iota(
        jnp.int32, (SEL, SEL), 1
    )
    inv64 = inv_freq((SEL, HD))

    def own_rope(c, carry):
        p = c * NS + s
        row = sel_ref[pl.ds(p, 1), :]
        col = jnp.sum(jnp.where(eye, jnp.broadcast_to(row, (SEL, SEL)), 0), axis=1, keepdims=True)
        pos = (col + offs[p]).astype(F32)
        cv, sv = rope_rows(pos * inv64)
        rc[c] = cv
        rsn[c] = sv
        return carry

    lax.fori_loop(0, CH, own_rope, 0)
    pos = lax.broadcasted_iota(jnp.int32, (PLEN, HD), 0).astype(F32)
    cosv, sinv = rope_rows(pos * inv_freq((PLEN, HD)))

    for cp in enc:
        cp.wait()
    summed = (
        eb[...].astype(F32) + er[0].astype(F32) + er[1].astype(F32) + er[2].astype(F32)
    )
    enc_k = rotate(summed[:, :HD], cosv, sinv).astype(BF)
    enc_v = summed[:, HD:].astype(BF)
    loads[3].wait()
    for i in range(POWN):
        miss = hit_ref[i] == 0
        zb[t * POWN + i, 0] = jnp.where(miss, enc_k, zb[t * POWN + i, 0])
        zb[t * POWN + i, 1] = jnp.where(miss, enc_v, zb[t * POWN + i, 1])

    def z_half(k, way, half):
        owner = lax.rem(t + 2 * NT - 2 * k if way == 0 else t + 2 * k, NT)
        return zb.at[pl.ds(owner * POWN + half * 2, 2)]

    def z_send(n, way):
        half = (n % 2) if way == 0 else 1 - (n % 2)
        ref = z_half(n // 2, way, half)
        return remote(ref, ref, zs.at[way, n], zr.at[way, n], zright if way == 0 else zleft)

    def z_recv(n, way):
        half = (n % 2) if way == 0 else 1 - (n % 2)
        ref = z_half(n // 2 + 1, way, half)
        return remote(ref, ref, zs.at[way, n], zr.at[way, n], zright if way == 0 else zleft)

    def to_sib(ref, i):
        return remote(ref, ref, ss.at[i], sr.at[i], sib)

    def sib_recv(ref, i):
        return remote(ref, ref, ss.at[i], sr.at[i], sib)

    sends = []
    sib_back = []
    sib_t = t + 1 - 2 * lax.rem(t, 2)

    def sib_ref(k, way, half):
        owner = lax.rem(sib_t + 2 * NT - 2 * k if way == 0 else sib_t + 2 * k, NT)
        return zb.at[pl.ds(owner * POWN + half * 2, 2)]

    for n in range(2):
        for way in range(2):
            cp = z_send(n, way)
            cp.start()
            sends.append(cp)
    for half in range(2):
        cp = to_sib(z_half(0, 0, half), half)
        cp.start()
        sends.append(cp)
        sib_back.append(sib_recv(sib_ref(0, 0, half), half))

    def z_service(n):
        for way in range(2):
            z_recv(n, way).wait_recv()
            half = (n % 2) if way == 0 else 1 - (n % 2)
            if n + 2 < 7:
                cp = z_send(n + 2, way)
                cp.start()
                sends.append(cp)
            i = 2 + 2 * n + way
            cp = to_sib(z_half(n // 2 + 1, way, half), i)
            cp.start()
            sends.append(cp)
            sib_back.append(sib_recv(sib_ref(n // 2 + 1, way, half), i))

    def p_send(c, d):
        rows = pl.ds(lax.rem(s + d, NS) * SEL, SEL)
        return remote(pb.at[c, rows], rb.at[c, d - 1], ps.at[c, d - 1], pr.at[c, d - 1], ydev(d))

    def project(c):
        def tile(n, carry):
            cols = pl.ds(pl.multiple_of(n * 256, 256), 256)
            total = jnp.zeros((CR, 256), F32)
            for slot, away in enumerate((0, 3, 1, 2)):
                owner = lax.rem(h + away, 4)
                wrows = pl.ds(pl.multiple_of(owner * FEAT, FEAT), FEAT)
                total += jnp.dot(
                    xb[slot, c * CR : (c + 1) * CR, :], wv[wrows, cols], preferred_element_type=F32
                )
            pb[c, :, cols] = total.astype(BF)
            return carry

        lax.fori_loop(0, COLS // 256, tile, 0)
        for d in (1, 2, 3):
            p_send(c, d).start()

    def f_send(c, d):
        slot = fb.at[c * NS + s]
        return remote(slot, slot, fs.at[c, d - 1], fr.at[c, d - 1], ydev(d))

    def f_recv(c, d):
        slot = fb.at[c * NS + lax.rem(s + NS - d, NS)]
        return remote(slot, slot, fs.at[c, d - 1], fr.at[c, d - 1], ydev(d))

    def finish_rows(c):
        for d in (1, 2, 3):
            p_send(c, d).wait()
        mine = pb[c, pl.ds(s * SEL, SEL), :].astype(F32)
        x = mine + rb[c, 0].astype(F32) + rb[c, 1].astype(F32) + rb[c, 2].astype(F32)
        x = x.astype(BF).astype(F32)
        cv, sv = rc[c], rsn[c]
        fb[c * NS + s, :, :HD] = rotate(x[:, G * HD : (G + 1) * HD], cv, sv).astype(BF)
        fb[c * NS + s, :, HD:] = x[:, (G + 1) * HD :].astype(BF)
        for d in (1, 2, 3):
            f_send(c, d).start()
        q = jnp.concatenate(
            [rotate(x[:, g * HD : (g + 1) * HD], cv, sv) for g in range(G)], axis=0
        )
        qb[c] = jnp.transpose(q).astype(BF)

    for c in range(CH):
        for cp in x_own(c):
            cp.wait()
        for cp in x_fwd(c):
            cp.start()
        if c + 2 < CH:
            for cp in x_own(c + 2):
                cp.start()
        if c >= 1:
            z_service(c - 1)
        for cp in x_fwd(c):
            cp.wait()
        project(c)
        if c >= 1:
            finish_rows(c - 1)
    z_service(3)
    finish_rows(CH - 1)
    for n in range(4, 7):
        z_service(n)
    for cp in sends:
        cp.wait_send()
    for cp in sib_back:
        cp.wait_recv()

    kio = lax.broadcasted_iota(jnp.int32, (PLEN, SEL), 0)
    kcol = lax.broadcasted_iota(jnp.int32, (PLEN, 1), 0)

    def build(j, carry):
        idx = loc_ref[pid_ref[t, j]]
        moved = rotate(zb[idx, 0].astype(F32), oc[pl.ds(j, 1), :], osn[pl.ds(j, 1), :])
        hot = (kio == sel_ref[pl.ds(j, 1), :]).astype(F32)
        chosen = jnp.max(hot, axis=1, keepdims=True) > 0.0
        fresh = jnp.dot(hot.astype(BF), fb[j], preferred_element_type=F32)
        ktab[j] = jnp.where(chosen, fresh[:, :HD], moved).astype(BF)
        vals = jnp.where(chosen, fresh[:, HD:], zb[idx, 1].astype(F32))
        vtab[j] = jnp.transpose(vals).astype(BF)
        return carry

    def o_copy(c, slot):
        return remote(ob.at[c], out_ref.at[slot], os_.at[c], or_.at[slot], {"serve": c})

    for c in range(CH):
        for d in (1, 2, 3):
            f_send(c, d).wait_send()
            f_recv(c, d).wait_recv()
        lax.fori_loop(c * NS, (c + 1) * NS, build, 0)
        p = c * NS + s
        qlim = jnp.concatenate([sel_ref[pl.ds(p, 1), :]] * G, axis=1)
        m_s[...] = jnp.full((1, G * SEL), -jnp.inf, F32)
        l_s[...] = jnp.zeros((1, G * SEL), F32)
        acc_s[...] = jnp.zeros((HD, G * SEL), F32)

        def tile(j, carry):
            sc = jnp.dot(ktab[j], qb[c], preferred_element_type=F32)
            lim = jnp.where(j < p, len_ref[pid_ref[t, j]] - 1, qlim)
            sc = jnp.where(kcol <= lim, sc, -jnp.inf)
            m_old = m_s[...]
            m_new = jnp.maximum(m_old, jnp.max(sc, axis=0, keepdims=True))
            alpha = jnp.exp2((m_old - m_new) * EXP_SCALE)
            e = jnp.exp2((sc - m_new) * EXP_SCALE)
            m_s[...] = m_new
            l_s[...] = l_s[...] * alpha + jnp.sum(e, axis=0, keepdims=True)
            acc_s[...] = acc_s[...] * alpha + jnp.dot(
                vtab[j], e.astype(BF), preferred_element_type=F32
            )
            return carry

        lax.fori_loop(0, p + 1, tile, 0)
        o = jnp.transpose(acc_s[...] / l_s[...])
        for g in range(G):
            ob[c, :, g * HD : (g + 1) * HD] = o[g * SEL : (g + 1) * SEL].astype(BF)

        @pl.when(s == c)
        def _():
            out_ref[c] = ob[c]

        @pl.when(s != c)
        def _():
            o_copy(c, s).start()

    for c in range(CH):

        @pl.when(s != c)
        def _():
            o_copy(c, s).wait_send()
            o_copy(c, c).wait_recv()


def local(
    passage_ids, location, passage_len, hit, sel_index, sel_hidden, miss_hidden, w_qkv, cache
):
    smem = pl.BlockSpec(memory_space=pltpu.SMEM)
    vmem = pl.BlockSpec(memory_space=pltpu.VMEM)
    hbm = pl.BlockSpec(memory_space=pl.ANY)
    dma = pltpu.SemaphoreType.DMA
    out = pl.pallas_call(
        kernel,
        out_shape=jax.ShapeDtypeStruct((NPAS // NS, SEL, G * HD), BF),
        in_specs=[smem, smem, smem, smem, vmem, hbm, hbm, hbm, hbm],
        out_specs=vmem,
        scratch_shapes=[
            pltpu.VMEM((4 * FEAT, COLS), BF),
            pltpu.VMEM((PLEN, 4 * FEAT), BF),
            pltpu.VMEM((4, ROWS, FEAT), BF),
            pltpu.VMEM((NT * POWN, 2, PLEN, HD), BF),
            pltpu.VMEM((PLEN, 2 * HD), BF),
            pltpu.VMEM((3, PLEN, 2 * HD), BF),
            pltpu.VMEM((CH, CR, COLS), BF),
            pltpu.VMEM((CH, 3, SEL, COLS), BF),
            pltpu.VMEM((NPAS, SEL, 2 * HD), BF),
            pltpu.VMEM((CH, HD, G * SEL), BF),
            pltpu.VMEM((NPAS, PLEN, HD), BF),
            pltpu.VMEM((NPAS, HD, PLEN), BF),
            pltpu.VMEM((CH, SEL, G * HD), BF),
            pltpu.SMEM((NPAS,), jnp.int32),
            pltpu.VMEM((NPAS, HD), F32),
            pltpu.VMEM((NPAS, HD), F32),
            pltpu.VMEM((CH, SEL, HD), F32),
            pltpu.VMEM((CH, SEL, HD), F32),
            pltpu.VMEM((HD, G * SEL), F32),
            pltpu.VMEM((1, G * SEL), F32),
            pltpu.VMEM((1, G * SEL), F32),
            dma((4,)),
            dma((4, CH)),
            dma((4, CH)),
            dma((3,)),
            dma((3,)),
            dma((2, 7)),
            dma((2, 7)),
            dma((16,)),
            dma((16,)),
            dma((CH, 3)),
            dma((CH, 3)),
            dma((CH, 3)),
            dma((CH, 3)),
            dma((CH,)),
            dma((NPAS // NS,)),
        ],
        compiler_params=pltpu.CompilerParams(
            collective_id=0, has_side_effects=True, vmem_limit_bytes=56 * 2**20
        ),
        cost_estimate=pl.CostEstimate(
            flops=10 * 10**9, bytes_accessed=9 * 2**20, transcendentals=8 * 2**20
        ),
        name="blended_attention",
    )(
        passage_ids,
        location,
        passage_len,
        hit,
        sel_index[0],
        sel_hidden[0],
        miss_hidden[0],
        w_qkv,
        cache,
    )
    return out[None]


def solution(mesh):
    in_specs = (
        P(),
        P(),
        P(),
        P("tier"),
        P("tier", None, None),
        P("tier", None, ("serve", "head")),
        P("tier", None, "serve"),
        P("serve", "head"),
        P("tier", None, None, "head"),
    )
    out_specs = P("tier", "serve", None, "head")
    return jax.shard_map(local, mesh=mesh, in_specs=in_specs, out_specs=out_specs, check_vma=False)
```

time: 229 us -> 99.2 us (0.43); the launches traced: 225 us -> 99 us
  Pallas kernels: 0 us -> 97.1 us
  waiting for transfers between devices: 84.2 us -> 0 us
  other arithmetic: 39.1 us -> 0 us
  local copies, waits for them, and re-layouts: 40 us -> 1.87 us
  matrix products: 33.4 us -> 0 us
  between operations: 15.3 us -> 0.01 us
  blocking collectives: 12.8 us -> 0 us
    pallas_call x0 -> x1, Pallas kernels: none -> 97.1 us  [local(): pl.pallas_call(kernel, out_shape=jax.ShapeDtypeStruct((NPAS // NS, SEL, G...]
    psum x1 -> x0, waiting for transfers between devices: 45.5 us -> none  [local(): lax.psum(partial_kv.astype(jnp.bfloat16), 'serve').astype(jnp.float32)]
    all_gather x2 -> x0, waiting for transfers between devices: 35.6 us -> none  [the longest x1 30.8 us: local(): shard_rows = lax.all_gather(kv_store, 'tier', axis=0, tiled=True)]
    dot_general x10 -> x0, matrix products: 33.4 us -> none  [the longest x4 10.9 us: attend(): jnp.einsum('hgqk,khd->qhgd', probs, value_rows, preferred_element_type=jn...]
    unnamed x26 -> x1, local copies, waits for them, and re-layouts: 18.8 us -> 1.87 us
    all_gather x1 -> x0, blocking collectives: 12.8 us -> none  [local(): fresh_all = lax.all_gather(fresh_pair, 'serve', axis=1, tiled=True)]
    gather x5 -> x0, local copies, waits for them, and re-layouts: 7.77 us -> none  [the longest x1 4.45 us: local(): picked = jnp.take(shard_rows, jnp.clip(wanted, 0, shard_len - 1), axis=0)]
    and x6 -> x0, other arithmetic: 6.38 us -> none  [the longest x4 6.35 us: local(): allowed = live[None, :] & (before | same_part)]
  transfers between devices with their start and end apart: 4 -> 0, of which waited for: 4 -> 0; matrix products, arithmetic and copies ran while one was open for 16% -> 0% of each run, Pallas kernels for 0% -> 0%
where the time goes in v1:
time: 99.2 us; the launch traced here: 99 us
  Pallas kernels  97.1 us (98%)
  local copies, waits for them, and re-layouts  1.87 us (2%)
    pallas_call x1, Pallas kernels, local(): pl.pallas_call(kernel, out_shape=jax.ShapeDtypeStruct((NPAS // NS, SEL, G...  97.1 us

profile of v1, /device:TPU:24, one launch (start us, length us, event | category | flops | bytes accessed | tf_op | source)
XLA Modules:
  0.0 99.0 jit_solution(5958062888944298708)
XLA Ops:
  0.0 97.1 %blended_attention.1 = bf16[4,64,1024]{2,1,0:T(8,128)(2,1)} custom-call(s32[16,16]{1,0:T(8,128)} %pid_ref.1, s32[64]{0:T(128)} %loc_ref.1, s32[64]{0:T(128)} %len_ref.1, s32[4]{0:T(128)} %hit_ref.1, s32[16,64]{1,0:T(8,128)} %bitcast.7, bf16[1024,512]{1,0:T(8,128)(2,1)} %bitcast.5, bf16[256,2048]{1,0:T(8,128)(2,1)} %bitcast.6, bf16[2048,1280]{1,0:T(8,128)(2,1)} %w_ref.1, ...), custom_call_target="tpu_custom_call" | custom-call | flops 10000000000 | bytes 9437184 | tf_op jit(solution)/shard_map/blended_attention/pallas_call | solution.py:347
  97.1 1.9 %copy.11 = bf16[1,4,64,1024]{3,2,1,0:T(8,128)(2,1)} copy(bf16[1,4,64,1024]{3,2,1,0:T(8,128)(2,1)} %bitcast.4) | data formatting | bytes 1048576

commit v2 on v1

v2 whole, which is shorter than its diff:
```python
import functools
import math

import jax
import jax.numpy as jnp
from jax import lax
from jax.experimental import pallas as pl
from jax.experimental.pallas import tpu as pltpu
from jax.sharding import PartitionSpec as P

HD = 128
G = 8
PLEN = 256
SEL = 64
NPAS = 16
POWN = 4
NT = 16
NS = 4
ROWS = NPAS * SEL
COLS = (G + 2) * HD
VR = HD + 16
CH = 8
CR = ROWS // CH
AHEAD = 2
SR = CR // NS
FEAT = 512
BF = jnp.bfloat16
F32 = jnp.float32
MESH = pl.DeviceIdType.MESH
LN_BASE = math.log(500000.0)
EXP_SCALE = math.log2(math.e) / math.sqrt(HD)


def remote(src, dst, ssem, rsem, target):
    return pltpu.make_async_remote_copy(
        src_ref=src, dst_ref=dst, send_sem=ssem, recv_sem=rsem, device_id=target, device_id_type=MESH
    )


def rope_rows(angle):
    lane = lax.broadcasted_iota(jnp.int32, angle.shape, 1)
    sine = jnp.sin(angle)
    return jnp.cos(angle), jnp.where(lane < HD // 2, -sine, sine)


def inv_freq(shape):
    lane = lax.broadcasted_iota(jnp.int32, shape, 1)
    half = jnp.where(lane < HD // 2, lane, lane - HD // 2).astype(F32)
    return jnp.exp(half * (-2.0 * LN_BASE / HD))


def rotate(x, c, s):
    return x * c + pltpu.roll(x, HD // 2, 1) * s


def kernel(
    pid_ref, loc_ref, len_ref, hit_ref, sel_ref, hid_ref, miss_ref, w_ref, cache_ref, out_ref,
    wv, mv, xb, cb, zb, hb, hsm, eb, er, pb, rb, fb, qb, ktab, vtab, ob, pos_s, offs, oc, osn, rc, rsn,
    acc_s, m_s,
    lsem, hs, hr, xs, xr, es, ers, zs, zr, ss, sr, ps, pr, fs, fr, os_, or_,
):
    t = lax.axis_index("tier")
    s = lax.axis_index("serve")
    h = lax.axis_index("head")
    sib = {"tier": t + 1 - 2 * lax.rem(t, 2)}
    zright = {"tier": lax.rem(t + 2, NT)}
    zleft = {"tier": lax.rem(t + NT - 2, NT)}
    xright = {"head": lax.rem(h + 1, 4)}
    xleft = {"head": lax.rem(h + 3, 4)}

    def ydev(d):
        return {"serve": lax.rem(s + d, NS)}

    loads = [
        pltpu.make_async_copy(hid_ref, xb.at[0], lsem.at[0]),
        pltpu.make_async_copy(miss_ref, mv, lsem.at[1]),
        pltpu.make_async_copy(w_ref, wv, lsem.at[2]),
        pltpu.make_async_copy(cache_ref, cb, lsem.at[3]),
    ]
    for cp in loads:
        cp.start()

    bar = pltpu.get_barrier_semaphore()
    tdev = [{"tier": lax.rem(t + d, NT)} for d in range(NT)]
    partners = [xright, xleft, ydev(1), ydev(2), ydev(3)] + tdev[1:]
    for dev in partners:
        pl.semaphore_signal(bar, inc=1, device_id=dev, device_id_type=MESH)
    pl.semaphore_wait(bar, len(partners))

    def x_own(c):
        rows = pl.ds(c * CR, CR)
        return (
            remote(xb.at[0, rows], xb.at[1, rows], xs.at[0, c], xr.at[0, c], xright),
            remote(xb.at[0, rows], xb.at[2, rows], xs.at[1, c], xr.at[1, c], xleft),
        )

    def x_fwd(c):
        a, b = pl.ds(c * CR, CR // 2), pl.ds(c * CR + CR // 2, CR // 2)
        return (
            remote(xb.at[1, a], xb.at[3, a], xs.at[2, c], xr.at[2, c], xright),
            remote(xb.at[2, b], xb.at[3, b], xs.at[3, c], xr.at[3, c], xleft),
        )

    loads[0].wait()
    for c in range(AHEAD):
        for cp in x_own(c):
            cp.start()

    missing = jnp.int32(0)
    for i in range(POWN):
        missing = missing + jnp.where(hit_ref[i] == 0, i, 0)
    hb[t] = jnp.full((1, HD), missing, jnp.int32)
    hits = [
        remote(hb.at[t], hb.at[t], hs.at[d - 1], hr.at[d - 1], tdev[d]) for d in range(1, NT)
    ]
    for cp in hits:
        cp.start()

    sib_t = t + 1 - 2 * lax.rem(t, 2)

    def z_block(me, k, way, q):
        owner = lax.rem(me + 2 * NT - 2 * k if way == 0 else me + 2 * k, NT)
        return zb.at[owner * POWN + q]

    def z_place(n, way):
        if n < 12:
            return n // 4 + 1, n % 4
        return 4, n - 12 + 2 * way

    def z_copy(k, q, way, n, ref):
        return remote(ref, ref, zs.at[way, n], zr.at[way, n], zright if way == 0 else zleft)

    sends = []
    sib_back = []

    def z_out(n, way):
        k, q = z_place(n, way)
        cp = z_copy(k, q, way, n, z_block(t, k - 1, way, q))
        cp.start()
        sends.append(cp)

    def to_sib(k, way, q, i):
        ref = z_block(t, k, way, q)
        cp = remote(ref, ref, ss.at[i], sr.at[i], sib)
        cp.start()
        sends.append(cp)
        back = z_block(sib_t, k, way, q)
        sib_back.append(remote(back, back, ss.at[i], sr.at[i], sib))

    def z_service(n):
        for way in range(2):
            k, q = z_place(n, way)
            z_copy(k, q, way, n, z_block(t, k, way, q)).wait_recv()
            if k < 3:
                z_out(n + 4, way)
            elif k == 3 and q // 2 == way:
                z_out(12 + q % 2, way)
            to_sib(k, way, q, 4 + 2 * n + way)

    loads[3].wait()
    for q in range(POWN - 1):
        zb[t * POWN + q] = cb[jnp.where(missing == q, POWN - 1, q)]
        for way in range(2):
            z_out(q, way)
    for q in range(POWN - 1):
        to_sib(0, 0, q, q)

    total = jnp.int32(0)
    row_id = lax.broadcasted_iota(jnp.int32, (NPAS, HD), 0)
    off_rows = jnp.zeros((NPAS, HD), jnp.int32)
    for j in range(NPAS):
        offs[j] = total
        off_rows = jnp.where(row_id == j, total, off_rows)
        total = total + len_ref[pid_ref[t, j]]
    cosv, sinv = rope_rows(off_rows.astype(F32) * inv_freq((NPAS, HD)))
    oc[...] = cosv
    osn[...] = sinv

    loads[1].wait()
    loads[2].wait()
    eb[...] = jnp.dot(mv[...], wv[:, G * HD :], preferred_element_type=F32).astype(BF)
    enc = [remote(eb, er.at[d - 1], es.at[d - 1], ers.at[d - 1], ydev(d)) for d in (1, 2, 3)]
    for cp in enc:
        cp.start()

    eye = lax.broadcasted_iota(jnp.int32, (SEL, SEL), 0) == lax.broadcasted_iota(
        jnp.int32, (SEL, SEL), 1
    )
    inv_rows = inv_freq((SR, HD))

    def own_rope(c, carry):
        p = 2 * c + lax.div(s, 2)
        row = sel_ref[pl.ds(p, 1), :]
        col = jnp.sum(jnp.where(eye, jnp.broadcast_to(row, (SEL, SEL)), 0), axis=1, keepdims=True)
        pos_s[...] = jnp.broadcast_to(col + offs[p], (SEL, HD))
        mine = pos_s[pl.ds(pl.multiple_of(lax.rem(s, 2) * SR, SR), SR), :]
        cv, sv = rope_rows(mine.astype(F32) * inv_rows)
        rc[c] = cv
        rsn[c] = sv
        return carry

    lax.fori_loop(0, CH, own_rope, 0)
    def finish_missing():
        pos = lax.broadcasted_iota(jnp.int32, (PLEN, HD), 0).astype(F32)
        cosv, sinv = rope_rows(pos * inv_freq((PLEN, HD)))
        for cp in enc:
            cp.wait()
        summed = eb[...].astype(F32) + er[0].astype(F32) + er[1].astype(F32) + er[2].astype(F32)
        zb[t * POWN + POWN - 1, 0] = rotate(summed[:, :HD], cosv, sinv).astype(BF)
        zb[t * POWN + POWN - 1, 1] = summed[:, HD:].astype(BF)
        for way in range(2):
            z_out(POWN - 1, way)
        to_sib(0, 0, POWN - 1, POWN - 1)

    def p_send(c, d):
        rows = pl.ds(lax.rem(s + d, NS) * SR, SR)
        return remote(pb.at[c, rows], rb.at[c, d - 1], ps.at[c, d - 1], pr.at[c, d - 1], ydev(d))

    def project(c):
        def tile(n, carry):
            cols = pl.ds(pl.multiple_of(n * 256, 256), 256)
            total = jnp.zeros((CR, 256), F32)
            for slot, away in enumerate((0, 3, 1, 2)):
                owner = lax.rem(h + away, 4)
                wrows = pl.ds(pl.multiple_of(owner * FEAT, FEAT), FEAT)
                total += jnp.dot(
                    xb[slot, c * CR : (c + 1) * CR, :], wv[wrows, cols], preferred_element_type=F32
                )
            pb[c, :, cols] = total.astype(BF)
            return carry

        lax.fori_loop(0, COLS // 256, tile, 0)
        for d in (1, 2, 3):
            p_send(c, d).start()

    def f_rows(c, who):
        return fb.at[pl.ds(pl.multiple_of(c * CR + who * SR, SR), SR)]

    def f_send(c, d):
        slot = f_rows(c, s)
        return remote(slot, slot, fs.at[c, d - 1], fr.at[c, d - 1], ydev(d))

    def f_recv(c, d):
        slot = f_rows(c, lax.rem(s + NS - d, NS))
        return remote(slot, slot, fs.at[c, d - 1], fr.at[c, d - 1], ydev(d))

    def finish_rows(c):
        for d in (1, 2, 3):
            p_send(c, d).wait()
        mine = pb[c, pl.ds(pl.multiple_of(s * SR, SR), SR), :].astype(F32)
        x = mine + rb[c, 0].astype(F32) + rb[c, 1].astype(F32) + rb[c, 2].astype(F32)
        x = x.astype(BF).astype(F32)
        cv, sv = rc[c], rsn[c]
        rows = pl.ds(pl.multiple_of(c * CR + s * SR, SR), SR)
        fb[rows, :HD] = rotate(x[:, G * HD : (G + 1) * HD], cv, sv).astype(BF)
        fb[rows, HD:] = x[:, (G + 1) * HD :].astype(BF)
        for d in (1, 2, 3):
            f_send(c, d).start()
        q = jnp.concatenate(
            [rotate(x[:, g * HD : (g + 1) * HD], cv, sv) for g in range(G)], axis=0
        )
        qb[c] = jnp.transpose(q).astype(BF)

    turns = ((), (0,), (1, 2), (3,), (4, 5), (6,), (7, 8), (9,), (10, 11))
    for i in range(CH + 1):
        if i < CH:
            for cp in x_own(i):
                cp.wait()
            for cp in x_fwd(i):
                cp.start()
            if i + AHEAD < CH:
                for cp in x_own(i + AHEAD):
                    cp.start()
        for n in turns[i]:
            z_service(n)
        if i >= 1:
            for cp in x_fwd(i - 1):
                cp.wait()
            project(i - 1)
        if i == 1:
            finish_missing()
        if i >= 2:
            finish_rows(i - 2)
    for n in (12, 13):
        z_service(n)
    for d in range(1, NT):
        hits[d - 1].wait_send()
        other = hb.at[lax.rem(t + NT - d, NT)]
        remote(other, other, hs.at[d - 1], hr.at[d - 1], tdev[d]).wait_recv()
    hit_copy = pltpu.make_async_copy(hb, hsm, lsem.at[0])
    hit_copy.start()
    for cp in sends:
        cp.wait_send()
    for cp in sib_back:
        cp.wait_recv()
    hit_copy.wait()

    kio = lax.broadcasted_iota(jnp.int32, (PLEN, SEL), 0)
    kcol = lax.broadcasted_iota(jnp.int32, (PLEN, 1), 0)
    count_row = lax.broadcasted_iota(jnp.int32, (VR - HD, PLEN), 0) == 0
    count_lane = lax.broadcasted_iota(jnp.int32, (VR - HD, PLEN), 1)

    def build(j, carry):
        pid = pid_ref[t, j]
        loc = loc_ref[pid]
        live = len_ref[pid]
        owner = lax.div(loc, POWN)
        slot = lax.rem(loc, POWN)
        gap = hsm[owner, 0, 0]
        place = jnp.where(slot == gap, POWN - 1, jnp.where(slot == POWN - 1, gap, slot))
        idx = owner * POWN + place
        half = pl.ds(pl.multiple_of(lax.rem(j, 2) * PLEN, PLEN), PLEN)
        pair = lax.div(j, 2)
        moved = rotate(zb[idx, 0].astype(F32), oc[pl.ds(j, 1), :], osn[pl.ds(j, 1), :])
        hot = (kio == sel_ref[pl.ds(j, 1), :]).astype(F32)
        chosen = jnp.max(hot, axis=1, keepdims=True) > 0.0
        rows = pl.ds(pl.multiple_of(j * SEL, SEL), SEL)
        fresh = jnp.dot(hot.astype(BF), fb[rows, :], preferred_element_type=F32)
        keys = jnp.where(chosen, fresh[:, :HD], moved)
        keys = jnp.where(kcol < live, keys, keys[0:1, :])
        ktab[pair, half, :] = keys.astype(BF)
        vals = jnp.where(chosen, fresh[:, HD:], zb[idx, 1].astype(F32))
        vals = jnp.where(kcol < live, vals, 0.0)
        vtab[pair, 0:HD, half] = jnp.transpose(vals).astype(BF)
        vtab[pair, HD:VR, half] = jnp.where(count_row & (count_lane < live), 1.0, 0.0).astype(BF)
        return carry

    def o_ref(c, who):
        rows = pl.ds(pl.multiple_of(lax.rem(who, 2) * SR, SR), SR)
        return out_ref.at[c % 2 * 2 + lax.div(who, 2), rows]

    def o_copy(c, who):
        return remote(ob.at[c], o_ref(c, who), os_.at[c], or_.at[c % 2, who], {"serve": c // 2})

    pcol = lax.broadcasted_iota(jnp.int32, (2 * PLEN, 1), 0)

    def soft_step(*steps):
        scores = [
            jnp.dot(ktab[pair], qb[c], preferred_element_type=F32) for c, pair, _ in steps
        ]
        for (c, pair, lim), sc in zip(steps, scores):
            if lim is not None:
                sc = jnp.where(pcol <= lim, sc, -jnp.inf)
            m_old = m_s[c % 2]
            m_new = jnp.maximum(m_old, jnp.max(sc, axis=0, keepdims=True))
            alpha = jnp.exp2((m_old - m_new) * EXP_SCALE)
            e = jnp.exp2((sc - m_new) * EXP_SCALE).astype(BF)
            m_s[c % 2] = m_new
            acc_s[c % 2] = acc_s[c % 2] * alpha + jnp.dot(
                vtab[pair], e, preferred_element_type=F32
            )

    def build_pair(c):
        for d in (1, 2, 3):
            f_send(c, d).wait_send()
            f_recv(c, d).wait_recv()
        lax.fori_loop(2 * c, 2 * c + 2, build, 0)

    late = lax.div(s, 2)

    def limits(c):
        row = sel_ref[pl.ds(2 * c + late, 1), :]
        lim = jnp.where(lax.rem(s, 2) == 0, row[:, :SR], row[:, SR:])
        return jnp.concatenate([lim] * G, axis=1) + late * PLEN

    def deliver(c):
        o = jnp.transpose(acc_s[c % 2, 0:HD, :] / acc_s[c % 2, HD : HD + 1, :])
        for g in range(G):
            ob[c, :, g * HD : (g + 1) * HD] = o[g * SR : (g + 1) * SR].astype(BF)

        @pl.when(s == c // 2)
        def _():
            rows = pl.ds(pl.multiple_of(lax.rem(s, 2) * SR, SR), SR)
            out_ref[c % 2 * 2 + lax.div(s, 2), rows, :] = ob[c]

        @pl.when(s != c // 2)
        def _():
            o_copy(c, s).start()

    def attend(a, before_last=None):
        b = a + 1
        m_s[...] = jnp.full((2, 1, G * SR), -jnp.inf, F32)
        acc_s[...] = jnp.zeros((2, VR, G * SR), F32)

        def both(pair, carry):
            soft_step((a, pair, None), (b, pair, None))
            return carry

        lax.fori_loop(0, a, both, 0)
        soft_step((a, a, limits(a)), (b, a, None))
        deliver(a)
        if before_last is not None:
            before_last()
        soft_step((b, b, limits(b)))
        deliver(b)

    for a in range(0, CH, 2):
        build_pair(a)
        if a == CH - 2:
            finish_rows(CH - 1)
        if a < CH - 2:
            build_pair(a + 1)
            attend(a)
        else:
            attend(a, lambda: build_pair(CH - 1))

    for c in range(CH):

        @pl.when(s != c // 2)
        def _():
            o_copy(c, s).wait_send()

    for c in range(2):
        for who in range(NS):

            @pl.when(s != who)
            def _():
                o_copy(c, who).wait_recv()


def local(
    passage_ids, location, passage_len, hit, sel_index, sel_hidden, miss_hidden, w_qkv, cache
):
    smem = pl.BlockSpec(memory_space=pltpu.SMEM)
    vmem = pl.BlockSpec(memory_space=pltpu.VMEM)
    hbm = pl.BlockSpec(memory_space=pl.ANY)
    dma = pltpu.SemaphoreType.DMA
    out = pl.pallas_call(
        kernel,
        out_shape=jax.ShapeDtypeStruct((NPAS // NS, SEL, G * HD), BF),
        in_specs=[smem, smem, smem, smem, vmem, hbm, hbm, hbm, hbm],
        out_specs=vmem,
        scratch_shapes=[
            pltpu.VMEM((4 * FEAT, COLS), BF),
            pltpu.VMEM((PLEN, 4 * FEAT), BF),
            pltpu.VMEM((4, ROWS, FEAT), BF),
            pltpu.VMEM((POWN, 2, PLEN, HD), BF),
            pltpu.VMEM((NT * POWN, 2, PLEN, HD), BF),
            pltpu.VMEM((NT, 1, HD), jnp.int32),
            pltpu.SMEM((NT, 1, HD), jnp.int32),
            pltpu.VMEM((PLEN, 2 * HD), BF),
            pltpu.VMEM((3, PLEN, 2 * HD), BF),
            pltpu.VMEM((CH, CR, COLS), BF),
            pltpu.VMEM((CH, 3, SR, COLS), BF),
            pltpu.VMEM((ROWS, 2 * HD), BF),
            pltpu.VMEM((CH, HD, G * SR), BF),
            pltpu.VMEM((NPAS // 2, 2 * PLEN, HD), BF),
            pltpu.VMEM((NPAS // 2, VR, 2 * PLEN), BF),
            pltpu.VMEM((CH, SR, G * HD), BF),
            pltpu.VMEM((SEL, HD), jnp.int32),
            pltpu.SMEM((NPAS,), jnp.int32),
            pltpu.VMEM((NPAS, HD), F32),
            pltpu.VMEM((NPAS, HD), F32),
            pltpu.VMEM((CH, SR, HD), F32),
            pltpu.VMEM((CH, SR, HD), F32),
            pltpu.VMEM((2, VR, G * SR), F32),
            pltpu.VMEM((2, 1, G * SR), F32),
            dma((4,)),
            dma((NT - 1,)),
            dma((NT - 1,)),
            dma((4, CH)),
            dma((4, CH)),
            dma((3,)),
            dma((3,)),
            dma((2, 14)),
            dma((2, 14)),
            dma((32,)),
            dma((32,)),
            dma((CH, 3)),
            dma((CH, 3)),
            dma((CH, 3)),
            dma((CH, 3)),
            dma((CH,)),
            dma((2, NS)),
        ],
        compiler_params=pltpu.CompilerParams(
            collective_id=0, has_side_effects=True, vmem_limit_bytes=56 * 2**20
        ),
        cost_estimate=pl.CostEstimate(
            flops=10 * 10**9, bytes_accessed=9 * 2**20, transcendentals=8 * 2**20
        ),
        name="blended_attention",
    )(
        passage_ids,
        location,
        passage_len,
        hit,
        sel_index[0],
        sel_hidden[0],
        miss_hidden[0],
        w_qkv,
        cache,
    )
    return out[None]


def solution(mesh):
    in_specs = (
        P(),
        P(),
        P(),
        P("tier"),
        P("tier", None, None),
        P("tier", None, ("serve", "head")),
        P("tier", None, "serve"),
        P("serve", "head"),
        P("tier", None, None, "head"),
    )
    out_specs = P("tier", "serve", None, "head")
    return jax.shard_map(local, mesh=mesh, in_specs=in_specs, out_specs=out_specs, check_vma=False)
```

time: 99.2 us -> 84.8 us (0.85)
  Pallas kernels: 97.1 us -> 82.4 us
    pallas_call x1, Pallas kernels: 97.1 us -> 82.4 us  [local(): pl.pallas_call(kernel, out_shape=jax.ShapeDtypeStruct((NPAS // NS, SEL, G...]
where the time goes in v2:
time: 84.8 us; the launch traced here: 84.3 us
  Pallas kernels  82.4 us (97%)
  local copies, waits for them, and re-layouts  1.87 us (2%)
    pallas_call x1, Pallas kernels, local(): pl.pallas_call(kernel, out_shape=jax.ShapeDtypeStruct((NPAS // NS, SEL, G...  82.4 us
    unnamed x1, local copies, waits for them, and re-layouts  1.87 us

profile of v2, /device:TPU:24, one launch (start us, length us, event | category | flops | bytes accessed | tf_op | source)
XLA Modules:
  0.0 84.3 jit_solution(11399340275485780142)
XLA Ops:
  0.0 82.4 %blended_attention.1 = bf16[4,64,1024]{2,1,0:T(8,128)(2,1)} custom-call(s32[16,16]{1,0:T(8,128)} %pid_ref.1, s32[64]{0:T(128)} %loc_ref.1, s32[64]{0:T(128)} %len_ref.1, s32[4]{0:T(128)} %hit_ref.1, s32[16,64]{1,0:T(8,128)} %bitcast.7, bf16[1024,512]{1,0:T(8,128)(2,1)} %bitcast.5, bf16[256,2048]{1,0:T(8,128)(2,1)} %bitcast.6, bf16[2048,1280]{1,0:T(8,128)(2,1)} %w_ref.1, ...), custom_call_target="tpu_custom_call" | custom-call | flops 10000000000 | bytes 9437184 | tf_op jit(solution)/shard_map/blended_attention/pallas_call | solution.py:428
  82.4 1.9 %copy.11 = bf16[1,4,64,1024]{3,2,1,0:T(8,128)(2,1)} copy(bf16[1,4,64,1024]{3,2,1,0:T(8,128)(2,1)} %bitcast.4) | data formatting | bytes 1048576

commit v3 on v2

--- a/solution.py
+++ b/solution.py
@@ -22,6 +22,7 @@
 CH = 8
 CR = ROWS // CH
 AHEAD = 2
+LAG = 3
 SR = CR // NS
 FEAT = 512
 BF = jnp.bfloat16
@@ -261,7 +262,7 @@
         )
         qb[c] = jnp.transpose(q).astype(BF)
 
-    turns = ((), (0,), (1, 2), (3,), (4, 5), (6,), (7, 8), (9,), (10, 11))
+    turns = ((), (0,), (1, 2), (3, 4), (5,), (6, 7), (8, 9), (10, 11), (12,))
     for i in range(CH + 1):
         if i < CH:
             for cp in x_own(i):
@@ -279,10 +280,12 @@
             project(i - 1)
         if i == 1:
             finish_missing()
-        if i >= 2:
-            finish_rows(i - 2)
-    for n in (12, 13):
-        z_service(n)
+        if i >= LAG:
+            finish_rows(i - LAG)
+    for c in range(CH - LAG + 1, CH - 1):
+        finish_rows(c)
+    z_service(13)
+    finish_rows(CH - 1)
     for d in range(1, NT):
         hits[d - 1].wait_send()
         other = hb.at[lax.rem(t + NT - d, NT)]
@@ -336,17 +339,17 @@
 
     def soft_step(*steps):
         scores = [
-            jnp.dot(ktab[pair], qb[c], preferred_element_type=F32) for c, pair, _ in steps
+            jnp.dot(ktab[pair], qb[c], preferred_element_type=F32) for _, c, pair, _ in steps
         ]
-        for (c, pair, lim), sc in zip(steps, scores):
+        for (slot, _, pair, lim), sc in zip(steps, scores):
             if lim is not None:
                 sc = jnp.where(pcol <= lim, sc, -jnp.inf)
-            m_old = m_s[c % 2]
+            m_old = m_s[slot]
             m_new = jnp.maximum(m_old, jnp.max(sc, axis=0, keepdims=True))
             alpha = jnp.exp2((m_old - m_new) * EXP_SCALE)
             e = jnp.exp2((sc - m_new) * EXP_SCALE).astype(BF)
-            m_s[c % 2] = m_new
-            acc_s[c % 2] = acc_s[c % 2] * alpha + jnp.dot(
+            m_s[slot] = m_new
+            acc_s[slot] = acc_s[slot] * alpha + jnp.dot(
                 vtab[pair], e, preferred_element_type=F32
             )
 
@@ -363,8 +366,8 @@
         lim = jnp.where(lax.rem(s, 2) == 0, row[:, :SR], row[:, SR:])
         return jnp.concatenate([lim] * G, axis=1) + late * PLEN
 
-    def deliver(c):
-        o = jnp.transpose(acc_s[c % 2, 0:HD, :] / acc_s[c % 2, HD : HD + 1, :])
+    def deliver(c, acc):
+        o = jnp.transpose(acc[0:HD, :] / acc[HD : HD + 1, :])
         for g in range(G):
             ob[c, :, g * HD : (g + 1) * HD] = o[g * SR : (g + 1) * SR].astype(BF)
 
@@ -377,32 +380,30 @@
         def _():
             o_copy(c, s).start()
 
-    def attend(a, before_last=None):
-        b = a + 1
-        m_s[...] = jnp.full((2, 1, G * SR), -jnp.inf, F32)
-        acc_s[...] = jnp.zeros((2, VR, G * SR), F32)
-
-        def both(pair, carry):
-            soft_step((a, pair, None), (b, pair, None))
+    def clear():
+        m_s[...] = jnp.full((8, 1, G * SR), -jnp.inf, F32)
+        acc_s[...] = jnp.zeros((8, VR, G * SR), F32)
+
+    def attend(first, last):
+        chunks = range(first, last + 1)
+        clear()
+
+        def common(pair, carry):
+            soft_step(*[(c - first, c, pair, None) for c in chunks])
             return carry
 
-        lax.fori_loop(0, a, both, 0)
-        soft_step((a, a, limits(a)), (b, a, None))
-        deliver(a)
-        if before_last is not None:
-            before_last()
-        soft_step((b, b, limits(b)))
-        deliver(b)
-
-    for a in range(0, CH, 2):
-        build_pair(a)
-        if a == CH - 2:
-            finish_rows(CH - 1)
-        if a < CH - 2:
-            build_pair(a + 1)
-            attend(a)
-        else:
-            attend(a, lambda: build_pair(CH - 1))
+        lax.fori_loop(0, first, common, 0)
+        for pair in chunks:
+            build_pair(pair)
+            soft_step(
+                *[
+                    (c - first, c, pair, limits(c) if c == pair else None)
+                    for c in range(pair, last + 1)
+                ]
+            )
+            deliver(pair, acc_s[pair - first])
+
+    attend(0, 7)
 
     for c in range(CH):
 
@@ -453,8 +454,8 @@
             pltpu.VMEM((NPAS, HD), F32),
             pltpu.VMEM((CH, SR, HD), F32),
             pltpu.VMEM((CH, SR, HD), F32),
-            pltpu.VMEM((2, VR, G * SR), F32),
-            pltpu.VMEM((2, 1, G * SR), F32),
+            pltpu.VMEM((8, VR, G * SR), F32),
+            pltpu.VMEM((8, 1, G * SR), F32),
             dma((4,)),
             dma((NT - 1,)),
             dma((NT - 1,)),

time: 84.8 us -> 81 us (0.955)
  Pallas kernels: 82.4 us -> 78.9 us
    pallas_call x1, Pallas kernels: 82.4 us -> 78.9 us  [local(): pl.pallas_call(kernel, out_shape=jax.ShapeDtypeStruct((NPAS // NS, SEL, G...]
where the time goes in v3:
time: 81 us; the launch traced here: 80.8 us
  Pallas kernels  78.9 us (97%)
  local copies, waits for them, and re-layouts  1.87 us (2%)
    pallas_call x1, Pallas kernels, local(): pl.pallas_call(kernel, out_shape=jax.ShapeDtypeStruct((NPAS // NS, SEL, G...  78.9 us
    unnamed x1, local copies, waits for them, and re-layouts  1.87 us

profile of v3, /device:TPU:24, one launch (start us, length us, event | category | flops | bytes accessed | tf_op | source)
XLA Modules:
  0.0 80.8 jit_solution(15026064901618931290)
XLA Ops:
  0.0 78.9 %blended_attention.1 = bf16[4,64,1024]{2,1,0:T(8,128)(2,1)} custom-call(s32[16,16]{1,0:T(8,128)} %pid_ref.1, s32[64]{0:T(128)} %loc_ref.1, s32[64]{0:T(128)} %len_ref.1, s32[4]{0:T(128)} %hit_ref.1, s32[16,64]{1,0:T(8,128)} %bitcast.7, bf16[1024,512]{1,0:T(8,128)(2,1)} %bitcast.5, bf16[256,2048]{1,0:T(8,128)(2,1)} %bitcast.6, bf16[2048,1280]{1,0:T(8,128)(2,1)} %w_ref.1, ...), custom_call_target="tpu_custom_call" | custom-call | flops 10000000000 | bytes 9437184 | tf_op jit(solution)/shard_map/blended_attention/pallas_call | solution.py:429
  78.9 1.9 %copy.11 = bf16[1,4,64,1024]{3,2,1,0:T(8,128)(2,1)} copy(bf16[1,4,64,1024]{3,2,1,0:T(8,128)(2,1)} %bitcast.4) | data formatting | bytes 1048576

commit v4 on v3

--- a/solution.py
+++ b/solution.py
@@ -200,7 +200,6 @@
         rsn[c] = sv
         return carry
 
-    lax.fori_loop(0, CH, own_rope, 0)
     def finish_missing():
         pos = lax.broadcasted_iota(jnp.int32, (PLEN, HD), 0).astype(F32)
         cosv, sinv = rope_rows(pos * inv_freq((PLEN, HD)))
@@ -272,12 +271,14 @@
             if i + AHEAD < CH:
                 for cp in x_own(i + AHEAD):
                     cp.start()
-        for n in turns[i]:
-            z_service(n)
+        if i == 0:
+            lax.fori_loop(0, CH, own_rope, 0)
         if i >= 1:
             for cp in x_fwd(i - 1):
                 cp.wait()
             project(i - 1)
+        for n in turns[i]:
+            z_service(n)
         if i == 1:
             finish_missing()
         if i >= LAG:
@@ -292,8 +293,6 @@
         remote(other, other, hs.at[d - 1], hr.at[d - 1], tdev[d]).wait_recv()
     hit_copy = pltpu.make_async_copy(hb, hsm, lsem.at[0])
     hit_copy.start()
-    for cp in sends:
-        cp.wait_send()
     for cp in sib_back:
         cp.wait_recv()
     hit_copy.wait()
@@ -404,6 +403,8 @@
             deliver(pair, acc_s[pair - first])
 
     attend(0, 7)
+    for cp in sends:
+        cp.wait_send()
 
     for c in range(CH):
 

time: 81 us -> 80.6 us (level)
  no operation moved by 1% of the time
where the time goes in v4:
time: 80.6 us; the launch traced here: 80.4 us
  Pallas kernels  78.5 us (97%)
  local copies, waits for them, and re-layouts  1.87 us (2%)
    pallas_call x1, Pallas kernels, local(): pl.pallas_call(kernel, out_shape=jax.ShapeDtypeStruct((NPAS // NS, SEL, G...  78.5 us
    unnamed x1, local copies, waits for them, and re-layouts  1.87 us

profile of v4, /device:TPU:24, one launch (start us, length us, event | category | flops | bytes accessed | tf_op | source)
XLA Modules:
  0.0 80.4 jit_solution(7111244062810471668)
XLA Ops:
  0.0 78.5 %blended_attention.1 = bf16[4,64,1024]{2,1,0:T(8,128)(2,1)} custom-call(s32[16,16]{1,0:T(8,128)} %pid_ref.1, s32[64]{0:T(128)} %loc_ref.1, s32[64]{0:T(128)} %len_ref.1, s32[4]{0:T(128)} %hit_ref.1, s32[16,64]{1,0:T(8,128)} %bitcast.7, bf16[1024,512]{1,0:T(8,128)(2,1)} %bitcast.5, bf16[256,2048]{1,0:T(8,128)(2,1)} %bitcast.6, bf16[2048,1280]{1,0:T(8,128)(2,1)} %w_ref.1, ...), custom_call_target="tpu_custom_call" | custom-call | flops 10000000000 | bytes 9437184 | tf_op jit(solution)/shard_map/blended_attention/pallas_call | solution.py:430
  78.5 1.9 %copy.11 = bf16[1,4,64,1024]{3,2,1,0:T(8,128)(2,1)} copy(bf16[1,4,64,1024]{3,2,1,0:T(8,128)(2,1)} %bitcast.4) | data formatting | bytes 1048576
